TPU v7x, 1024 devices: a whole 8x8x8 slice. The times are simulated.
1024 devices in a mesh: row: 16 (over y, core), col: 64 (over z, x).
Axes of the slice: x: 8, y: 8, z: 8, core: 2. Of those that a mesh axis runs over, the one named last changes fastest.
Arguments:
- features: bfloat16 [655360, 128], P(('row', 'col')), may hold values from -6 to 6
- send_blocks: int32 [16, 64, 16, 2], P('row', 'col'), may hold values from -1 to 4, as said below
- tile_slots: int32 [16, 64, 20, 4], P('row', 'col'), may hold values from 0 to 31, as said below
- tile_count: int32 [16, 64, 20], P('row', 'col'), may hold values from 1 to 4, as said below
- adjacency: bfloat16 [16, 64, 20, 128, 512], P('row', 'col'), may hold values from -0.25 to 0.25
- w_self: bfloat16 [128, 256], replicated, may hold values from -0.5 to 0.5
- w_neigh: bfloat16 [128, 256], replicated, may hold values from -0.5 to 0.5
- bias: float32 [256], replicated, may hold values from -3 to 3
Outputs:
- hidden: bfloat16 [655360, 256], P(('row', 'col'))
Inputs may be any that keep to these rules, and one draw needn't show every extreme that they name: `send_blocks`: each (owner, reader) pair has 1 to 2 live slots, first in order, holding distinct blocks of the owner; the rest are -1; every owner has 2 live slots for some reader. `tile_slots`: each entry names a live slot q * 2 + s of the need-list that owner (q, c) keeps for this device's row on the same col. `tile_count`: every device has a destination block with 4 live tiles.
All inputs are finite; a program needn't handle non-finite values.
Results may differ from a plain program's by a relative error of at most 0.0043.
Values may be sent and summed in bfloat16 or wider, within the bound.
No kernel may reach another device: no remote copies, remote signals or barrier semaphores. Data moves between devices by JAX's collectives and lax.ppermute only.
A program may use at most 32 MiB of HBM per device.

v0:
```python
import jax
import jax.numpy as jnp
from jax import lax
from jax.sharding import PartitionSpec as P


def passed_along(value, axis, steps):
    count = lax.axis_size(axis)
    pairs = [(source, (source + steps) % count) for source in range(count)]
    return lax.ppermute(value, axis, pairs)


def shards(features, send_blocks, tile_slots, tile_count, adjacency, w_self, w_neigh, bias):
    row_count = lax.axis_size("row")
    tile_rows = adjacency.shape[3]
    per_dst = tile_slots.shape[3]
    width = features.shape[1]
    own_blocks = features.shape[0] // tile_rows
    band_len = adjacency.shape[2] // own_blocks
    blocks = features.reshape(own_blocks, tile_rows, width)
    block_ids = send_blocks[0, 0]
    need_from = lax.all_to_all(block_ids, "row", split_axis=0, concat_axis=0, tiled=True)
    gathered = lax.all_gather(blocks, "row", axis=0, tiled=True)
    position = jnp.arange(row_count, dtype=jnp.int32)[:, None] * own_blocks + jnp.clip(
        need_from, 0, own_blocks - 1
    )
    source = gathered[position.reshape(-1)]
    slot_ids = tile_slots[0, 0]
    counts = tile_count[0, 0]
    adjacent = adjacency[0, 0]
    keep_mask = jnp.arange(per_dst, dtype=jnp.int32)[None, :] < counts[:, None]

    def panel_of(k):
        lower = k * own_blocks
        upper = lower + own_blocks
        operand = jnp.where(
            keep_mask[lower:upper][:, :, None, None],
            source[slot_ids[lower:upper]],
            jnp.zeros((), jnp.bfloat16),
        )
        operand = operand.reshape(own_blocks, per_dst * tile_rows, width)
        product = jnp.einsum(
            "bim,bmf->bif", adjacent[lower:upper], operand, preferred_element_type=jnp.float32
        )
        return product.reshape(own_blocks * tile_rows, width)

    summed = panel_of(0)
    for k in range(1, band_len):
        summed = summed + passed_along(panel_of(k), "col", k)
    aggregate = summed.astype(jnp.bfloat16)
    pre_act = jnp.dot(features, w_self, preferred_element_type=jnp.float32)
    pre_act = pre_act + jnp.dot(aggregate, w_neigh, preferred_element_type=jnp.float32) + bias
    return jax.nn.relu(pre_act).astype(jnp.bfloat16)


def solution(mesh):
    return jax.shard_map(
        shards,
        mesh=mesh,
        in_specs=(
            P(("row", "col"), None),
            P("row", "col", None, None),
            P("row", "col", None, None),
            P("row", "col", None),
            P("row", "col", None, None, None),
            P(),
            P(),
            P(),
        ),
        out_specs=P(("row", "col"), None),
        check_vma=False,
    )
```

profile of v0, /device:TPU:1, one launch (start us, length us, event | category | flops | bytes accessed | tf_op | source)
XLA Modules:
  0.0 134.2 jit_solution(7816463859683450826)
XLA Ops:
  6.5 0.0 copy-start
  6.5 0.0 all-gather.2.cloned.1.call-start
  6.5 0.7 all-gather.2.cloned.1.call-update
  7.3 1.4 %copy.19 = s32[16,1,2]{2,1,0:T(1,128)} copy(s32[16,1,2]{0,2,1:T(2,128)} %bitcast.102) | data formatting | bytes 256 | tf_op jit(solution)/shard_map/all_to_all | solution.py:22
  8.6 17.4 %all-to-all-start = ((s32[16,1,2]{2,1,0:T(1,128)}), s32[16,1,2]{2,1,0:T(1,128)S(1)}, u32[]{:S(2)}, u32[]{:S(2)}) async-start(s32[16,1,2]{2,1,0:T(1,128)} %copy.19), calls=%async_computation | async-start | bytes 16384 | tf_op jit(solution)/shard_map/all_to_all | solution.py:22
  26.0 0.7 iota_compare_fusion
  26.8 0.1 broadcast_bitcast_fusion.2
  26.9 0.1 add.91
  26.9 0.1 add.92
  27.0 0.9 compare_select_fusion.3
  27.9 0.1 copy.21
  28.0 0.1 reshape.219
  28.1 0.1 broadcast_bitcast_fusion
  28.2 0.1 copy.22
  28.3 0.1 reshape.227
  28.4 0.1 copy.23
  28.5 0.1 reshape.235
  28.6 0.1 copy.20
  28.7 0.1 reshape.211
  28.8 0.0 copy-done
  28.8 1.1 fusion.20
  30.0 3.0 %all-to-all-done = s32[16,1,2]{2,1,0:T(1,128)S(1)} async-done(((s32[16,1,2]{2,1,0:T(1,128)}), s32[16,1,2]{2,1,0:T(1,128)S(1)}, u32[]{:S(2)}, u32[]{:S(2)}) %all-to-all-start) | async-done | bytes 160 | tf_op jit(solution)/shard_map/all_to_all | solution.py:22
  33.0 0.1 min.12
  33.2 35.0 %all-gather.2.cloned.1.call-done = bf16[80,128,128]{2,1,0:T(8,128)(2,1)} async-done(((bf16[5,128,128]{2,1,0:T(8,128)(2,1)}), bf16[80,128,128]{2,1,0:T(8,128)(2,1)}) %all-gather.2.cloned.1.call-update) | async-done | bytes 2621456 | tf_op jit(solution)/shard_map/all_gather | solution.py:23
  68.2 2.5 %gather_fusion = bf16[32,128,128]{2,1,0:T(8,128)(2,1)S(1)} fusion(bf16[80,128,128]{2,1,0:T(8,128)(2,1)} %all-gather.2.cloned.1.call-done, s32[1024]{0:T(1024)S(1)} %pad_clamp_fusion.4), kind=kCustom, calls=%fused_computation | custom fusion | bytes 2097280 | tf_op jit(solution)/shard_map/gather | solution.py:27
  70.6 0.7 gather_fusion.2
  71.3 0.5 bitcast_select_fusion.2
  71.9 1.4 %fusion.7 = f32[5,128,128]{1,2,0:T(8,128)S(1)} fusion(bf16[5,512,128]{2,1,0:T(8,128)(2,1)S(1)} %bitcast_select_fusion.2, bf16[1,1,20,128,512]{4,3,2,1,0:T(8,128)(2,1)} %param.12), kind=kOutput, calls=%fused_computation.15 | convolution fusion | flops 83886080 | bytes 1638400 | tf_op jit(solution)/shard_map/bim,bmf->bif/dot_general | solution.py:42
  73.3 3.1 %collective-permute-start = (f32[640,128]{1,0:T(8,128)S(1)}, f32[640,128]{1,0:T(8,128)S(1)}, u32[]{:S(2)}, u32[]{:S(2)}) collective-permute-start(f32[640,128]{1,0:T(8,128)S(1)} %bitcast.97), channel_id=1, source_target_pairs={{0,1},{1,2},{2,3},{3,4},{4,5},{5,6},{6,7},{7,8},{8,9},{9,10},{10,1... | collective-permute-start | bytes 983048 | tf_op jit(solution)/shard_map/ppermute | solution.py:10
  76.4 0.7 gather_fusion.3
  77.1 0.5 bitcast_select_fusion.1
  77.6 2.1 %fusion.5 = f32[5,128,128]{1,2,0:T(8,128)} fusion(bf16[5,512,128]{2,1,0:T(8,128)(2,1)S(1)} %bitcast_select_fusion.1, bf16[1,1,20,128,512]{4,3,2,1,0:T(8,128)(2,1)} %param.12), kind=kOutput, calls=%fused_computation.12 | convolution fusion | flops 83886080 | bytes 1638400 | tf_op jit(solution)/shard_map/bim,bmf->bif/dot_general | solution.py:42
  79.8 4.0 %collective-permute-start.1 = (f32[640,128]{1,0:T(8,128)}, f32[640,128]{1,0:T(8,128)S(1)}, u32[]{:S(2)}, u32[]{:S(2)}) collective-permute-start(f32[640,128]{1,0:T(8,128)} %bitcast.18), channel_id=1, source_target_pairs={{0,2},{1,3},{2,4},{3,5},{4,6},{5,7},{6,8},{7,9},{8,10},{9,11},{10,... | collective-permute-start | bytes 983048 | tf_op jit(solution)/shard_map/ppermute | solution.py:10
  83.8 0.7 gather_fusion.4
  84.4 0.5 bitcast_select_fusion
  85.0 2.1 %fusion.3 = f32[5,128,128]{1,2,0:T(8,128)} fusion(bf16[5,512,128]{2,1,0:T(8,128)(2,1)S(1)} %bitcast_select_fusion, bf16[1,1,20,128,512]{4,3,2,1,0:T(8,128)(2,1)} %param.12), kind=kOutput, calls=%fused_computation.9 | convolution fusion | flops 83886080 | bytes 1638400 | tf_op jit(solution)/shard_map/bim,bmf->bif/dot_general | solution.py:42
  87.1 0.0 copy-start.1
  87.1 0.0 copy-start.2
  87.1 4.4 %collective-permute-start.2 = (f32[640,128]{1,0:T(8,128)}, f32[640,128]{1,0:T(8,128)}, u32[]{:S(2)}, u32[]{:S(2)}) collective-permute-start(f32[640,128]{1,0:T(8,128)} %bitcast.23), channel_id=1, source_target_pairs={{0,3},{1,4},{2,5},{3,6},{4,7},{5,8},{6,9},{7,10},{8,11},{9,12},{10... | collective-permute-start | bytes 983048 | tf_op jit(solution)/shard_map/ppermute | solution.py:10
  91.6 0.7 gather_fusion.1
  92.2 0.5 bitcast_select_fusion.3
  92.8 1.4 %fusion.9 = f32[5,128,128]{1,2,0:T(8,128)S(1)} fusion(bf16[5,512,128]{2,1,0:T(8,128)(2,1)S(1)} %bitcast_select_fusion.3, bf16[1,1,20,128,512]{4,3,2,1,0:T(8,128)(2,1)} %param.12), kind=kOutput, calls=%fused_computation.18 | convolution fusion | flops 83886080 | bytes 1638400 | tf_op jit(solution)/shard_map/bim,bmf->bif/dot_general | solution.py:42
  94.2 0.0 collective-permute-done
  94.2 6.1 %collective-permute-done.1 = f32[640,128]{1,0:T(8,128)S(1)} collective-permute-done((f32[640,128]{1,0:T(8,128)}, f32[640,128]{1,0:T(8,128)S(1)}, u32[]{:S(2)}, u32[]{:S(2)}) %collective-permute-start.1) | collective-permute-done | bytes 327712 | tf_op jit(solution)/shard_map/ppermute | solution.py:10
  100.3 25.0 %collective-permute-done.2 = f32[640,128]{1,0:T(8,128)} collective-permute-done((f32[640,128]{1,0:T(8,128)}, f32[640,128]{1,0:T(8,128)}, u32[]{:S(2)}, u32[]{:S(2)}) %collective-permute-start.2) | collective-permute-done | bytes 327712 | tf_op jit(solution)/shard_map/ppermute | solution.py:10
  125.3 1.0 fusion.17
  126.3 0.0 copy-done.1
  126.3 0.0 copy-done.2
  126.3 1.0 fusion.2
  (13 shorter events, 0.1 us)
Async XLA Ops:
  6.5 22.3 %copy-start = (bf16[128,256]{1,0:T(8,128)(2,1)S(1)}, bf16[128,256]{1,0:T(8,128)(2,1)}, u32[]{:S(2)}) copy-start(bf16[128,256]{1,0:T(8,128)(2,1)} %param.13) | copy-start | bytes 196612
  6.5 61.6 %all-gather.2.cloned.1.call-start = ((), (), s32[]{:S(2)}) async-start(), calls=%async_computation.1 | async-start | bytes 2785280 | tf_op jit(solution)/shard_map/all_gather | solution.py:23
  8.6 24.4 %all-to-all-start = ((s32[16,1,2]{2,1,0:T(1,128)}), s32[16,1,2]{2,1,0:T(1,128)S(1)}, u32[]{:S(2)}, u32[]{:S(2)}) async-start(s32[16,1,2]{2,1,0:T(1,128)} %copy.19), calls=%async_computation | async-start | bytes 16384 | tf_op jit(solution)/shard_map/all_to_all | solution.py:22
  73.3 20.9 %collective-permute-start = (f32[640,128]{1,0:T(8,128)S(1)}, f32[640,128]{1,0:T(8,128)S(1)}, u32[]{:S(2)}, u32[]{:S(2)}) collective-permute-start(f32[640,128]{1,0:T(8,128)S(1)} %bitcast.97), channel_id=1, source_target_pairs={{0,1},{1,2},{2,3},{3,4},{4,5},{5,6},{6,7},{7,8},{8,9},{9,10},{10,1... | collective-permute-start | bytes 983048 | tf_op jit(solution)/shard_map/ppermute | solution.py:10
  79.8 20.5 %collective-permute-start.1 = (f32[640,128]{1,0:T(8,128)}, f32[640,128]{1,0:T(8,128)S(1)}, u32[]{:S(2)}, u32[]{:S(2)}) collective-permute-start(f32[640,128]{1,0:T(8,128)} %bitcast.18), channel_id=1, source_target_pairs={{0,2},{1,3},{2,4},{3,5},{4,6},{5,7},{6,8},{7,9},{8,10},{9,11},{10,... | collective-permute-start | bytes 983048 | tf_op jit(solution)/shard_map/ppermute | solution.py:10
  87.1 39.2 %copy-start.1 = (bf16[128,256]{1,0:T(8,128)(2,1)S(1)}, bf16[128,256]{1,0:T(8,128)(2,1)}, u32[]{:S(2)}) copy-start(bf16[128,256]{1,0:T(8,128)(2,1)} %param.14) | copy-start | bytes 196612
  87.1 39.2 %copy-start.2 = (f32[256]{0:T(256)S(1)}, f32[256]{0:T(256)}, u32[]{:S(2)}) copy-start(f32[256]{0:T(256)} %param.15) | copy-start | bytes 3076
  87.1 38.2 %collective-permute-start.2 = (f32[640,128]{1,0:T(8,128)}, f32[640,128]{1,0:T(8,128)}, u32[]{:S(2)}, u32[]{:S(2)}) collective-permute-start(f32[640,128]{1,0:T(8,128)} %bitcast.23), channel_id=1, source_target_pairs={{0,3},{1,4},{2,5},{3,6},{4,7},{5,8},{6,9},{7,10},{8,11},{9,12},{10... | collective-permute-start | bytes 983048 | tf_op jit(solution)/shard_map/ppermute | solution.py:10
Sparse Core Ops, SparseCore 0:
  10.1 58.0 all-gather.1
where the time goes:
time: 135 us; the launch traced here: 134 us
  waiting for transfers between devices  69.9 us (52%)
  starting transfers between devices  29 us (21%)
  between operations  13.6 us (10%)
  matrix products  9.21 us (7%)
  local copies, waits for them, and re-layouts  7.68 us (6%)
  other arithmetic  4.79 us (4%)
    all_gather x1, waiting for transfers between devices, shards(): gathered = lax.all_gather(blocks, 'row', axis=0, tiled=True)  35 us
    ppermute x3, waiting for transfers between devices, passed_along(): return lax.ppermute(value, axis, pairs)  31.1 us
    all_to_all x1, starting transfers between devices, shards(): lax.all_to_all(block_ids, 'row', split_axis=0, concat_axis=0, tiled=True)  17.4 us
    ppermute x3, starting transfers between devices, passed_along(): return lax.ppermute(value, axis, pairs)  11.5 us
    dot_general x4, matrix products, panel_of(): jnp.einsum('bim,bmf->bif', adjacent[lower:upper], operand, preferred_elem...  7.12 us
    all_to_all x1, waiting for transfers between devices, shards(): lax.all_to_all(block_ids, 'row', split_axis=0, concat_axis=0, tiled=True)  3.05 us
  transfers between devices with their start and end apart: 5, of which 4 were waited for; matrix products, arithmetic and copies ran while one was open for 11% of the time, Pallas kernels for 0%

commit v1 on v0

v1 whole, which is shorter than its diff:
```python
import functools

import jax
import jax.numpy as jnp
from jax import lax
from jax.experimental import pallas as pl
from jax.experimental.pallas import tpu as pltpu
from jax.sharding import PartitionSpec as P

SCALE = 8192.0


def passed_along(value, axis, steps):
    count = lax.axis_size(axis)
    pairs = [(source, (source + steps) % count) for source in range(count)]
    return lax.ppermute(value, axis, pairs)


def tile_products(first, count, per_dst, rows, slots_ref, place_ref, x_ref, adj_ref, write):
    for b in range(count):
        tiles = []
        for j in range(per_dst):
            slot = slots_ref[(first + b) * per_dst + j]
            start = pl.multiple_of(place_ref[jnp.maximum(slot, 0)], 16)
            tile = x_ref[pl.ds(start, rows), :]
            tiles.append(jnp.where(slot >= 0, tile, jnp.zeros_like(tile)))
        operand = jnp.concatenate(tiles, axis=0)
        product = jnp.dot(adj_ref[first + b], operand, preferred_element_type=jnp.float32)
        write(b, product * (1.0 / SCALE))


def last_kernel(own, band, per_dst, rows, slots_ref, place_ref, x_ref, adj_ref, far_ref):
    def write(b, product):
        far_ref[b * rows : (b + 1) * rows, :] = product.astype(far_ref.dtype)

    tile_products((band - 1) * own, own, per_dst, rows, slots_ref, place_ref, x_ref, adj_ref, write)


def rest_kernel(own, band, per_dst, rows, slots_ref, place_ref, x_ref, adj_ref, mine_ref, near_ref, mid_ref):
    for k, out_ref in ((1, near_ref), (2, mid_ref), (0, mine_ref)):

        def write(b, product, out_ref=out_ref):
            out_ref[b * rows : (b + 1) * rows, :] = product.astype(out_ref.dtype)

        tile_products(k * own, own, per_dst, rows, slots_ref, place_ref, x_ref, adj_ref, write)


def final_kernel(self_ref, mine_ref, near_ref, far_ref, w_ref, bias_ref, out_ref):
    summed = mine_ref[...] + near_ref[...].astype(jnp.float32) + far_ref[...].astype(jnp.float32)
    pre_act = jnp.dot(summed.astype(jnp.bfloat16), w_ref[...], preferred_element_type=jnp.float32)
    pre_act = pre_act + self_ref[...] + bias_ref[...]
    out_ref[...] = jnp.maximum(pre_act, 0.0).astype(out_ref.dtype)


def shards(features, send_blocks, tile_slots, tile_count, adjacency, w_self, w_neigh, bias):
    row_count = lax.axis_size("row")
    readers, cap = send_blocks.shape[2:]
    tile_rows = adjacency.shape[3]
    per_dst = tile_slots.shape[3]
    nodes, width = features.shape
    own = nodes // tile_rows
    band = adjacency.shape[2] // own
    assert band == 4

    scaled = (features.astype(jnp.float32) * SCALE).astype(jnp.float16)
    listed = jnp.pad(send_blocks[0, 0].astype(jnp.float16), ((0, 0), (0, width - cap)))
    held = nodes + readers
    got = lax.all_gather(jnp.concatenate([scaled, listed], axis=0), "row", axis=0, tiled=True)
    reader = lax.axis_index("row")
    need = lax.dynamic_slice(got.reshape(row_count, held, width), (0, nodes + reader, 0), (row_count, 1, cap))
    need = jnp.clip(need.reshape(row_count, cap).astype(jnp.int32), 0, own - 1)
    place = jnp.arange(row_count, dtype=jnp.int32)[:, None] * held + need * tile_rows
    place = place.reshape(row_count * cap)
    live = jnp.arange(per_dst, dtype=jnp.int32)[None, :] < tile_count[0, 0][:, None]
    slots = jnp.where(live, tile_slots[0, 0], -1).reshape(-1)
    source = got.astype(jnp.bfloat16)
    adjacent = adjacency[0, 0]

    smem = pl.BlockSpec(memory_space=pltpu.SMEM)
    vmem = pl.BlockSpec(memory_space=pltpu.VMEM)
    part = functools.partial
    tile_flops = 2 * tile_rows * tile_rows * per_dst * width
    far = pl.pallas_call(
        part(last_kernel, own, band, per_dst, tile_rows),
        out_shape=jax.ShapeDtypeStruct((nodes, width), jnp.bfloat16),
        in_specs=[smem, smem, vmem, vmem],
        out_specs=vmem,
        cost_estimate=pl.CostEstimate(flops=own * tile_flops, bytes_accessed=2**20, transcendentals=0),
    )(slots, place, source, adjacent)
    far = passed_along(far, "col", 1)
    mine, near, mid = pl.pallas_call(
        part(rest_kernel, own, band, per_dst, tile_rows),
        out_shape=[
            jax.ShapeDtypeStruct((nodes, width), jnp.float32),
            jax.ShapeDtypeStruct((nodes, width), jnp.bfloat16),
            jax.ShapeDtypeStruct((nodes, width), jnp.float32),
        ],
        in_specs=[smem, smem, vmem, vmem],
        out_specs=[vmem, vmem, vmem],
        cost_estimate=pl.CostEstimate(flops=3 * own * tile_flops, bytes_accessed=3 * 2**20, transcendentals=0),
    )(slots, place, source, adjacent)
    near = passed_along(near, "col", 1)
    far = passed_along((far.astype(jnp.float32) + mid).astype(jnp.bfloat16), "col", 2)
    own_part = jnp.dot(features, w_self, preferred_element_type=jnp.float32)
    return pl.pallas_call(
        final_kernel,
        out_shape=jax.ShapeDtypeStruct((nodes, w_self.shape[1]), jnp.bfloat16),
        in_specs=[vmem] * 6,
        out_specs=vmem,
    )(own_part, mine, near, far, w_neigh, bias.reshape(1, -1))


def solution(mesh):
    return jax.shard_map(
        shards,
        mesh=mesh,
        in_specs=(
            P(("row", "col"), None),
            P("row", "col", None, None),
            P("row", "col", None, None),
            P("row", "col", None),
            P("row", "col", None, None, None),
            P(),
            P(),
            P(),
        ),
        out_specs=P(("row", "col"), None),
        check_vma=False,
    )
```

time: 135 us -> 78.8 us (0.58)
  waiting for transfers between devices: 69.9 us -> 15.5 us
  blocking collectives: 0 us -> 39.2 us
  starting transfers between devices: 29 us -> 5.87 us
  between operations: 13.6 us -> 0.09 us
  Pallas kernels: 0 us -> 9.85 us
  matrix products: 9.21 us -> 1.07 us
  local copies, waits for them, and re-layouts: 7.68 us -> 1.34 us
    all_gather x0 -> x1, blocking collectives: none -> 39.2 us  [shards(): lax.all_gather(jnp.concatenate([scaled, listed], axis=0), 'row', axis=0,...]
    all_gather x1 -> x0, waiting for transfers between devices: 35 us -> none  [shards(): gathered = lax.all_gather(blocks, 'row', axis=0, tiled=True)]
    all_to_all x1 -> x0, starting transfers between devices: 17.4 us -> none  [shards(): lax.all_to_all(block_ids, 'row', split_axis=0, concat_axis=0, tiled=True)]
    ppermute x3, waiting for transfers between devices: 31.1 us -> 15.5 us  [passed_along(): return lax.ppermute(value, axis, pairs)]
    pallas_call x0 -> x3, Pallas kernels: none -> 9.85 us  [the longest x1 4.02 us: shards(): pl.pallas_call(part(rest_kernel, own, band, per_dst, tile_rows), out_shap...]
    dot_general x6 -> x1, matrix products: 9.21 us -> 1.07 us  [shards(): own_part = jnp.dot(features, w_self, preferred_element_type=jnp.float32)]
    ppermute x3, starting transfers between devices: 11.5 us -> 5.87 us  [passed_along(): return lax.ppermute(value, axis, pairs)]
    gather x5 -> x0, local copies, waits for them, and re-layouts: 5.18 us -> none  [the longest x4 2.69 us: panel_of(): source[slot_ids[lower:upper]]]
  transfers between devices with their start and end apart: 5 -> 3, of which waited for: 4 -> 3; matrix products, arithmetic and copies ran while one was open for 11% -> 3% of each run, Pallas kernels for 0% -> 5%
where the time goes in v1:
time: 78.8 us; the launch traced here: 78.5 us
  blocking collectives  39.2 us (50%)
  waiting for transfers between devices  15.5 us (20%)
  Pallas kernels  9.85 us (12%)
  starting transfers between devices  5.87 us (7%)
  other arithmetic  5.6 us (7%)
  local copies, waits for them, and re-layouts  1.34 us (2%)
  matrix products  1.07 us (1%)
    all_gather x1, blocking collectives, shards(): lax.all_gather(jnp.concatenate([scaled, listed], axis=0), 'row', axis=0,...  39.2 us
    ppermute x3, waiting for transfers between devices, passed_along(): return lax.ppermute(value, axis, pairs)  15.5 us
    ppermute x3, starting transfers between devices, passed_along(): return lax.ppermute(value, axis, pairs)  5.87 us
    pallas_call x1, Pallas kernels, shards(): pl.pallas_call(part(rest_kernel, own, band, per_dst, tile_rows), out_shap...  4.02 us
    pallas_call x1, Pallas kernels, shards(): pl.pallas_call(part(last_kernel, own, band, per_dst, tile_rows), out_shap...  3.58 us
    pallas_call x1, Pallas kernels, shards(): pl.pallas_call(final_kernel, out_shape=jax.ShapeDtypeStruct((nodes, w_sel...  2.25 us
    convert_element_type x1, other arithmetic, shards(): source = got.astype(jnp.bfloat16)  1.67 us
  transfers between devices with their start and end apart: 3, of which 3 were waited for; matrix products, arithmetic and copies ran while one was open for 3% of the time, Pallas kernels for 5%

profile of v1, /device:TPU:1, one launch (start us, length us, event | category | flops | bytes accessed | tf_op | source)
XLA Modules:
  0.0 78.5 jit_solution(17782856206873525758)
XLA Ops:
  0.0 0.0 copy-start
  0.0 1.0 %multiply_convert_fusion = f16[640,128]{1,0:T(8,128)(2,1)S(1)} fusion(bf16[640,128]{1,0:T(8,128)(2,1)} %param.8), kind=kLoop, calls=%fused_computation.3 | loop fusion | flops 245760 | bytes 327680 | tf_op jit(solution)/shard_map/convert_element_type | solution.py:65
  1.0 0.7 convert_bitcast_fusion
  1.7 0.1 copy.13
  1.8 39.2 %all-gather.1 = f16[10496,128]{1,0:T(8,128)(2,1)S(1)} all-gather(f16[656,128]{1,0:T(8,128)(2,1)S(1)} %fusion.1), channel_id=1, replica_groups=mesh['row'=16,'col'=64] {'row'}, dimensions={0}, use_global_device_ids=true | all-gather | bytes 2854912 | tf_op jit(solution)/shard_map/all_gather | solution.py:68
  41.0 0.0 copy-start.4
  41.0 0.0 copy-start.5
  41.0 1.7 %convert_element_type.33.x_ref = bf16[10496,128]{1,0:T(8,128)(2,1)} convert(f16[10496,128]{1,0:T(8,128)(2,1)S(1)} %all-gather.1) | non-fusion elementwise | flops 1343488 | bytes 5373952 | tf_op jit(solution)/shard_map/convert_element_type | solution.py:76
  42.7 0.1 mul.29
  42.8 0.1 add.21
  42.9 0.1 add.22
  43.0 0.0 copy-done.4
  43.0 0.1 copy.12
  43.1 0.1 squeeze.7
  43.2 0.0 copy-done.5
  43.2 0.1 iota_compare_fusion.1
  43.3 0.1 lt.26
  43.4 0.5 add.24.place_ref
  43.9 0.6 broadcast_select_fusion.slots_ref
  44.5 3.6 %shard_map.83 = bf16[640,128]{1,0:T(8,128)(2,1)} custom-call(s32[80]{0:T(128)} %broadcast_select_fusion.slots_ref, s32[32]{0:T(128)} %add.24.place_ref, bf16[10496,128]{1,0:T(8,128)(2,1)} %convert_element_type.33.x_ref, bf16[20,128,512]{2,1,0:T(8,128)(2,1)} %bitcast.11), custom_call_target="tpu_custom_call" | custom-call | flops 83886080 | bytes 1048576 | tf_op jit(solution)/shard_map/pallas_call | solution.py:83
  48.1 0.0 copy-start.1
  48.1 2.0 %collective-permute-start.1 = (bf16[640,128]{1,0:T(8,128)(2,1)}, bf16[640,128]{1,0:T(8,128)(2,1)S(1)}, u32[]{:S(2)}, u32[]{:S(2)}) collective-permute-start(bf16[640,128]{1,0:T(8,128)(2,1)} %shard_map.83), channel_id=1, source_target_pairs={{0,1},{1,2},{2,3},{3,4},{4,5},{5,6},{6,7},{7,8},{8,9},{9,10},{10,1... | collective-permute-start | bytes 491528 | tf_op jit(solution)/shard_map/ppermute | solution.py:16
  50.1 4.0 %shard_map.82 = (f32[640,128]{1,0:T(8,128)}, bf16[640,128]{1,0:T(8,128)(2,1)}, f32[640,128]{1,0:T(8,128)}) custom-call(s32[80]{0:T(128)} %broadcast_select_fusion.slots_ref, s32[32]{0:T(128)} %add.24.place_ref, bf16[10496,128]{1,0:T(8,128)(2,1)} %convert_element_type.33.x_ref, bf16[20,128,512]{2,1,0:T(8,128)(2,1)} %bitcast.12), custom_call_target="tpu_custom_call" | custom-call | flops 251658240 | bytes 3145728 | tf_op jit(solution)/shard_map/pallas_call | solution.py:91
  54.1 1.9 %collective-permute-start = (bf16[640,128]{1,0:T(8,128)(2,1)}, bf16[640,128]{1,0:T(8,128)(2,1)S(1)}, u32[]{:S(2)}, u32[]{:S(2)}) collective-permute-start(bf16[640,128]{1,0:T(8,128)(2,1)} %get-tuple-element.9), channel_id=1, source_target_pairs={{0,1},{1,2},{2,3},{3,4},{4,5},{5,6},{6,7},{7,8},{8,9},{9,10},{10,1... | collective-permute-start | bytes 491528 | tf_op jit(solution)/shard_map/ppermute | solution.py:16
  56.0 4.8 %collective-permute-done.1 = bf16[640,128]{1,0:T(8,128)(2,1)S(1)} collective-permute-done((bf16[640,128]{1,0:T(8,128)(2,1)}, bf16[640,128]{1,0:T(8,128)(2,1)S(1)}, u32[]{:S(2)}, u32[]{:S(2)}) %collective-permute-start.1) | collective-permute-done | bytes 163872 | tf_op jit(solution)/shard_map/ppermute | solution.py:16
  60.8 1.0 %add_convert_fusion = bf16[640,128]{1,0:T(8,128)(2,1)S(1)} fusion(f32[640,128]{1,0:T(8,128)} %get-tuple-element.10, bf16[640,128]{1,0:T(8,128)(2,1)S(1)} %collective-permute-done.1), kind=kLoop, calls=%fused_computation.2 | loop fusion | flops 245760 | bytes 655360 | tf_op jit(solution)/shard_map/convert_element_type | solution.py:103
  61.9 1.9 %collective-permute-start.2 = (bf16[640,128]{1,0:T(8,128)(2,1)S(1)}, bf16[640,128]{1,0:T(8,128)(2,1)S(1)}, u32[]{:S(2)}, u32[]{:S(2)}) collective-permute-start(bf16[640,128]{1,0:T(8,128)(2,1)S(1)} %add_convert_fusion), channel_id=1, source_target_pairs={{0,2},{1,3},{2,4},{3,5},{4,6},{5,7},{6,8},{7,9},{8,10},{9,11},{10,... | collective-permute-start | bytes 491528 | tf_op jit(solution)/shard_map/ppermute | solution.py:16
  63.8 0.0 copy-done
  63.8 0.0 copy-done.1
  63.8 1.1 %fusion.2.self_ref = f32[640,256]{1,0:T(8,128)} fusion(bf16[640,128]{1,0:T(8,128)(2,1)S(1)} %copy-done.1, bf16[128,256]{1,0:T(8,128)(2,1)S(1)} %copy-done), kind=kOutput, calls=%fused_computation.11 | convolution fusion | flops 41943040 | bytes 884736 | tf_op jit(solution)/shard_map/dot_general | solution.py:104
  64.9 1.9 %collective-permute-done.near_ref = bf16[640,128]{1,0:T(8,128)(2,1)S(1)} collective-permute-done((bf16[640,128]{1,0:T(8,128)(2,1)}, bf16[640,128]{1,0:T(8,128)(2,1)S(1)}, u32[]{:S(2)}, u32[]{:S(2)}) %collective-permute-start) | collective-permute-done | bytes 163872 | tf_op jit(solution)/shard_map/ppermute | solution.py:16
  66.8 0.0 copy-start.2
  66.8 8.7 %collective-permute-done.2.far_ref = bf16[640,128]{1,0:T(8,128)(2,1)S(1)} collective-permute-done((bf16[640,128]{1,0:T(8,128)(2,1)S(1)}, bf16[640,128]{1,0:T(8,128)(2,1)S(1)}, u32[]{:S(2)}, u32[]{:S(2)}) %collective-permute-start.2) | collective-permute-done | bytes 163872 | tf_op jit(solution)/shard_map/ppermute | solution.py:16
  75.5 0.0 copy-start.3
  75.5 0.0 copy-done.2
  75.5 0.7 copy-done.3
  76.2 2.3 %shard_map.84 = bf16[640,256]{1,0:T(8,128)(2,1)} custom-call(f32[640,256]{1,0:T(8,128)} %fusion.2.self_ref, f32[640,128]{1,0:T(8,128)} %get-tuple-element.8.mine_ref, bf16[640,128]{1,0:T(8,128)(2,1)} %copy-done.2, bf16[640,128]{1,0:T(8,128)(2,1)} %copy-done.3, bf16[128,256]{1,0:T(8,128)(2,1)} %w_ref.1, f32[1,256]{1,0:T(1,128)} %bitcast.13), custom_call_target="tpu_custom_call" | custom-call | tf_op jit(solution)/shard_map/pallas_call | solution.py:105
  (4 shorter events, 0.1 us)
Async XLA Ops:
  0.0 63.8 %copy-start = (bf16[128,256]{1,0:T(8,128)(2,1)S(1)}, bf16[128,256]{1,0:T(8,128)(2,1)}, u32[]{:S(2)}) copy-start(bf16[128,256]{1,0:T(8,128)(2,1)} %param.13) | copy-start | bytes 196612
  41.0 2.0 %copy-start.4 = (s32[1,1,20,4]{2,3,1,0:T(4,128)S(1)}, s32[1,1,20,4]{2,3,1,0:T(4,128)}, u32[]{:S(2)}) copy-start(s32[1,1,20,4]{2,3,1,0:T(4,128)} %param.10) | copy-start | bytes 964
  41.0 2.2 %copy-start.5 = (s32[1,1,20]{2,1,0:T(1,128)S(1)}, s32[1,1,20]{2,1,0:T(1,128)}, u32[]{:S(2)}) copy-start(s32[1,1,20]{2,1,0:T(1,128)} %param.11) | copy-start | bytes 244
  48.1 15.7 %copy-start.1 = (bf16[640,128]{1,0:T(8,128)(2,1)S(1)}, bf16[640,128]{1,0:T(8,128)(2,1)}, u32[]{:S(2)}) copy-start(bf16[640,128]{1,0:T(8,128)(2,1)} %param.8) | copy-start | bytes 491524
  48.1 12.8 %collective-permute-start.1 = (bf16[640,128]{1,0:T(8,128)(2,1)}, bf16[640,128]{1,0:T(8,128)(2,1)S(1)}, u32[]{:S(2)}, u32[]{:S(2)}) collective-permute-start(bf16[640,128]{1,0:T(8,128)(2,1)} %shard_map.83), channel_id=1, source_target_pairs={{0,1},{1,2},{2,3},{3,4},{4,5},{5,6},{6,7},{7,8},{8,9},{9,10},{10,1... | collective-permute-start | bytes 491528 | tf_op jit(solution)/shard_map/ppermute | solution.py:16
  54.1 12.7 %collective-permute-start = (bf16[640,128]{1,0:T(8,128)(2,1)}, bf16[640,128]{1,0:T(8,128)(2,1)S(1)}, u32[]{:S(2)}, u32[]{:S(2)}) collective-permute-start(bf16[640,128]{1,0:T(8,128)(2,1)} %get-tuple-element.9), channel_id=1, source_target_pairs={{0,1},{1,2},{2,3},{3,4},{4,5},{5,6},{6,7},{7,8},{8,9},{9,10},{10,1... | collective-permute-start | bytes 491528 | tf_op jit(solution)/shard_map/ppermute | solution.py:16
  61.9 13.7 %collective-permute-start.2 = (bf16[640,128]{1,0:T(8,128)(2,1)S(1)}, bf16[640,128]{1,0:T(8,128)(2,1)S(1)}, u32[]{:S(2)}, u32[]{:S(2)}) collective-permute-start(bf16[640,128]{1,0:T(8,128)(2,1)S(1)} %add_convert_fusion), channel_id=1, source_target_pairs={{0,2},{1,3},{2,4},{3,5},{4,6},{5,7},{6,8},{7,9},{8,10},{9,11},{10,... | collective-permute-start | bytes 491528 | tf_op jit(solution)/shard_map/ppermute | solution.py:16
  66.8 8.7 %copy-start.2 = (bf16[640,128]{1,0:T(8,128)(2,1)}, bf16[640,128]{1,0:T(8,128)(2,1)S(1)}, u32[]{:S(2)}) copy-start(bf16[640,128]{1,0:T(8,128)(2,1)S(1)} %collective-permute-done.near_ref) | copy-start | bytes 491524
  75.5 0.7 copy-start.3

commit v2 on v0

v2 whole, which is shorter than its diff:
```python
import functools

import jax
import jax.numpy as jnp
from jax import lax
from jax.experimental import pallas as pl
from jax.experimental.pallas import tpu as pltpu
from jax.sharding import PartitionSpec as P

SCALE = 8192.0
PART_SCALE = 32.0
VMEM_LIMIT = 8 * 2**20


def passed_along(value, axis, steps):
    count = lax.axis_size(axis)
    pairs = [(source, (source + steps) % count) for source in range(count)]
    return lax.ppermute(value, axis, pairs)


def pack_kernel(last, features_ref, listed_ref, slots_ref, counts_ref, adj_ref, out_ref, plan_ref, adj_out, listed, slots, counts, turned, arrived):
    nodes = features_ref.shape[0]
    cap, readers = listed_ref.shape
    per_dst, blocks = slots_ref.shape
    copies = []
    for source, target in (
        (listed_ref, listed),
        (slots_ref, slots),
        (counts_ref, counts),
        (features_ref, out_ref.at[pl.ds(0, nodes)]),
        (adj_ref.at[pl.ds(last, blocks - last)], adj_out),
    ):
        copy = pltpu.make_async_copy(source, target, arrived.at[len(copies)])
        copy.start()
        copies.append(copy)
    turned[...] = jnp.zeros_like(turned)
    for copy in copies[:3]:
        copy.wait()
    plan_ref[:per_dst, :] = slots[...]
    plan_ref[per_dst:, :] = counts[...]
    turned[:cap, :readers] = listed[...].astype(jnp.float32)
    out_ref[nodes:, :] = jnp.transpose(turned[...])[:readers, :].astype(out_ref.dtype)
    for copy in copies[3:]:
        copy.wait()


def band_kernel(ks, first, own, rows, held, plan_ref, need_ref, x_ref, adj_ref, *rest):
    *outs, operand = rest
    per_dst = plan_ref.shape[0] - 1
    cap = need_ref.shape[1]
    for k, out_ref in zip(ks, outs, strict=True):
        for b in range(own):
            block = k * own + b
            for j in range(per_dst):
                slot = plan_ref[j, block]
                owner = lax.div(slot, cap)
                wanted = jnp.clip(need_ref[owner, lax.rem(slot, cap)], 0, own - 1)
                start = pl.multiple_of(owner * held + wanted * rows, 16)
                tile = x_ref[pl.ds(start, rows), :]
                tile = jnp.where(j < plan_ref[per_dst, block], tile, jnp.zeros_like(tile))
                operand[b, j * rows : (j + 1) * rows, :] = tile
        for b in range(own):
            product = jnp.dot(adj_ref[k * own + b - first], operand[b], preferred_element_type=jnp.float32)
            out_ref[b * rows : (b + 1) * rows, :] = product * (PART_SCALE / SCALE)


def final_kernel(self_ref, *rest):
    *parts, w_ref, bias_ref, out_ref = rest
    summed = parts[0][...]
    for part in parts[1:]:
        summed = summed + part[...]
    aggregate = (summed * (1.0 / PART_SCALE)).astype(jnp.bfloat16)
    pre_act = jnp.dot(aggregate, w_ref[...], preferred_element_type=jnp.float32)
    pre_act = pre_act + self_ref[...] + bias_ref[...]
    out_ref[...] = jnp.maximum(pre_act, 0.0).astype(out_ref.dtype)


def in_hbm(value):
    return pltpu.with_memory_space_constraint(value, pltpu.HBM)


def in_vmem(value):
    return pltpu.with_memory_space_constraint(value, pltpu.VMEM)


def shards(features, send_blocks, tile_slots, tile_count, adjacency, w_self, w_neigh, bias):
    row_count = lax.axis_size("row")
    readers, cap = send_blocks.shape[2:]
    rows = adjacency.shape[3]
    per_dst = tile_slots.shape[3]
    nodes, width = features.shape
    own = nodes // rows
    band = adjacency.shape[2] // own
    assert band == 4
    smem = pl.BlockSpec(memory_space=pltpu.SMEM)
    vmem = pl.BlockSpec(memory_space=pltpu.VMEM)
    anywhere = pl.BlockSpec(memory_space=pl.ANY)
    params = pltpu.CompilerParams(vmem_limit_bytes=VMEM_LIMIT)

    held = nodes + readers
    last = (band - 1) * own
    adjacent = adjacency[0, 0]
    packed, plan, adjacent_last = pl.pallas_call(
        functools.partial(pack_kernel, last),
        out_shape=[
            pltpu.VMEM((held, width), jnp.bfloat16),
            pltpu.VMEM((per_dst + 1, band * own), jnp.int32),
            pltpu.VMEM((own, *adjacent.shape[1:]), jnp.bfloat16),
        ],
        in_specs=[anywhere] * 5,
        out_specs=[vmem] * 3,
        scratch_shapes=[
            pltpu.VMEM((cap, readers), jnp.int32),
            pltpu.VMEM((per_dst, band * own), jnp.int32),
            pltpu.VMEM((1, band * own), jnp.int32),
            pltpu.VMEM((width, width), jnp.float32),
            pltpu.SemaphoreType.DMA((5,)),
        ],
        compiler_params=params,
    )(in_hbm(features), in_hbm(send_blocks[0, 0].T), in_hbm(tile_slots[0, 0].T), in_hbm(tile_count[0]), in_hbm(adjacent))
    sent = (packed.astype(jnp.float32) * SCALE).astype(jnp.float16)
    got = lax.all_gather(sent, "row", axis=0, tiled=True)
    source = got.astype(jnp.bfloat16)
    reader = lax.axis_index("row")
    need = lax.dynamic_slice(source.reshape(row_count, held, width), (0, nodes + reader, 0), (row_count, 1, cap))
    need = (need.reshape(row_count, cap).astype(jnp.float32) * (1.0 / SCALE)).astype(jnp.int32)
    tile_flops = 2 * rows * rows * per_dst * width

    def products(ks, matrices, first):
        count = len(ks) * own
        return pl.pallas_call(
            functools.partial(band_kernel, ks, first, own, rows, held),
            out_shape=[pltpu.VMEM((nodes, width), jnp.float32)] * len(ks),
            in_specs=[smem, smem, vmem, vmem],
            out_specs=[vmem] * len(ks),
            scratch_shapes=[pltpu.VMEM((own, per_dst * rows, width), jnp.bfloat16)],
            compiler_params=params,
            cost_estimate=pl.CostEstimate(flops=count * tile_flops, bytes_accessed=len(ks) * 2**20, transcendentals=0),
        )(plan, need, in_vmem(source), in_vmem(matrices))

    (far,) = products((3,), adjacent_last, last)
    far = passed_along(far.astype(jnp.float16), "col", 1)
    (near,) = products((1,), adjacent, 0)
    near = passed_along(near.astype(jnp.float16), "col", 1)
    mid, mine = products((2, 0), adjacent, 0)
    far = passed_along((far.astype(jnp.float32) + mid).astype(jnp.float16), "col", 2)
    parts = (mine, near.astype(jnp.float32), far.astype(jnp.float32))
    own_part = jnp.dot(features, w_self, preferred_element_type=jnp.float32)
    return pl.pallas_call(
        final_kernel,
        out_shape=jax.ShapeDtypeStruct((nodes, w_self.shape[1]), jnp.bfloat16),
        in_specs=[vmem] * (len(parts) + 3),
        out_specs=vmem,
        compiler_params=params,
    )(in_vmem(own_part), *[in_vmem(p) for p in parts], in_vmem(w_neigh), in_vmem(bias.reshape(1, -1)))


def solution(mesh):
    return jax.shard_map(
        shards,
        mesh=mesh,
        in_specs=(
            P(("row", "col"), None),
            P("row", "col", None, None),
            P("row", "col", None, None),
            P("row", "col", None),
            P("row", "col", None, None, None),
            P(),
            P(),
            P(),
        ),
        out_specs=P(("row", "col"), None),
        check_vma=False,
    )
```

time: 135 us -> 69.3 us (0.51)
  waiting for transfers between devices: 69.9 us -> 16.5 us
  blocking collectives: 0 us -> 39.2 us
  starting transfers between devices: 29 us -> 5.89 us
  between operations: 13.6 us -> 0.18 us
  matrix products: 9.21 us -> 0.22 us
  local copies, waits for them, and re-layouts: 7.68 us -> 0.23 us
  Pallas kernels: 0 us -> 6.39 us
  other arithmetic: 4.79 us -> 0.52 us
    all_gather x0 -> x1, blocking collectives: none -> 39.2 us  [shards(): got = lax.all_gather(sent, 'row', axis=0, tiled=True)]
    all_gather x1 -> x0, waiting for transfers between devices: 35 us -> none  [shards(): gathered = lax.all_gather(blocks, 'row', axis=0, tiled=True)]
    all_to_all x1 -> x0, starting transfers between devices: 17.4 us -> none  [shards(): lax.all_to_all(block_ids, 'row', split_axis=0, concat_axis=0, tiled=True)]
    ppermute x3, waiting for transfers between devices: 31.1 us -> 16.5 us  [passed_along(): return lax.ppermute(value, axis, pairs)]
    dot_general x6 -> x1, matrix products: 9.21 us -> 0.22 us  [shards(): own_part = jnp.dot(features, w_self, preferred_element_type=jnp.float32)]
    pallas_call x0 -> x5, Pallas kernels: none -> 6.39 us  [the longest x3 4.11 us: products(): pl.pallas_call(functools.partial(band_kernel, ks, first, own, rows, held)...]
    ppermute x3, starting transfers between devices: 11.5 us -> 5.89 us  [passed_along(): return lax.ppermute(value, axis, pairs)]
    gather x5 -> x0, local copies, waits for them, and re-layouts: 5.18 us -> none  [the longest x4 2.69 us: panel_of(): source[slot_ids[lower:upper]]]
  transfers between devices with their start and end apart: 5 -> 3, of which waited for: 4 -> 3; matrix products, arithmetic and copies ran while one was open for 11% -> 0% of each run, Pallas kernels for 0% -> 4%
where the time goes in v2:
time: 69.3 us; the launch traced here: 69.1 us
  blocking collectives  39.2 us (57%)
  waiting for transfers between devices  16.5 us (24%)
  Pallas kernels  6.39 us (9%)
  starting transfers between devices  5.89 us (8%)
    all_gather x1, blocking collectives, shards(): got = lax.all_gather(sent, 'row', axis=0, tiled=True)  39.2 us
    ppermute x3, waiting for transfers between devices, passed_along(): return lax.ppermute(value, axis, pairs)  16.5 us
    ppermute x3, starting transfers between devices, passed_along(): return lax.ppermute(value, axis, pairs)  5.89 us
    pallas_call x3, Pallas kernels, products(): pl.pallas_call(functools.partial(band_kernel, ks, first, own, rows, held)...  4.11 us
  transfers between devices with their start and end apart: 3, of which 3 were waited for; matrix products, arithmetic and copies ran while one was open for 0% of the time, Pallas kernels for 4%

profile of v2, /device:TPU:1, one launch (start us, length us, event | category | flops | bytes accessed | tf_op | source)
XLA Modules:
  0.0 69.1 jit_solution(8519308191588881763)
XLA Ops:
  0.0 0.0 copy-start
  0.0 1.3 %shard_map.82 = (bf16[656,128]{1,0:T(8,128)(2,1)S(1)}, s32[5,20]{1,0:T(8,128)S(1)}, bf16[5,128,512]{2,1,0:T(8,128)(2,1)S(1)}) custom-call(bf16[640,128]{1,0:T(8,128)(2,1)} %features_ref.1, s32[2,16]{1,0:T(2,128)} %bitcast.20, s32[4,20]{1,0:T(4,128)} %bitcast.19, s32[1,20]{1,0:T(1,128)} %bitcast.21, bf16[20,128,512]{2,1,0:T(8,128)(2,1)} %bitcast.15), custom_call_target="tpu_custom_call" | custom-call | tf_op jit(solution)/shard_map/pallas_call | solution.py:103
  1.4 39.2 %all-gather.1 = f16[10496,128]{1,0:T(8,128)(2,1)S(1)} all-gather(f16[656,128]{1,0:T(8,128)(2,1)S(1)} %multiply_convert_fusion), channel_id=1, replica_groups=mesh['row'=16,'col'=64] {'row'}, dimensions={0}, use_global_device_ids=true | all-gather | bytes 2854912 | tf_op jit(solution)/shard_map/all_gather | solution.py:122
  40.5 0.3 convert_element_type.38.x_ref
  40.9 0.1 copy.13
  41.0 0.1 copy.10.need_ref
  41.1 0.0 copy-start.1
  41.1 1.2 %shard_map.85 = f32[640,128]{1,0:T(8,128)S(1)} custom-call(s32[5,20]{1,0:T(8,128)S(1)} %get-tuple-element.10.plan_ref, s32[16,2]{1,0:T(8,128)S(1)} %copy.10.need_ref, bf16[10496,128]{1,0:T(8,128)(2,1)S(1)} %convert_element_type.38.x_ref, bf16[5,128,512]{2,1,0:T(8,128)(2,1)S(1)} %get-tuple-element.13.adj_ref), custom_call_target="tpu_custom_call" | custom-call | flops 83886080 | bytes 1048576 | tf_op jit(solution)/shard_map/pallas_call | solution.py:131
  42.4 1.9 %collective-permute-start.1 = (f16[640,128]{1,0:T(8,128)(2,1)S(1)}, f16[640,128]{1,0:T(8,128)(2,1)S(1)}, u32[]{:S(2)}, u32[]{:S(2)}) collective-permute-start(f16[640,128]{1,0:T(8,128)(2,1)S(1)} %convert_element_type.44), channel_id=1, source_target_pairs={{0,1},{1,2},{2,3},{3,4},{4,5},{5,6},{6,7},{7,8},{8,9},{9,10},{10,1... | collective-permute-start | bytes 491528 | tf_op jit(solution)/shard_map/ppermute | solution.py:18
  44.3 0.0 copy-done.1
  44.3 1.2 %shard_map.84 = f32[640,128]{1,0:T(8,128)S(1)} custom-call(s32[5,20]{1,0:T(8,128)S(1)} %get-tuple-element.10.plan_ref, s32[16,2]{1,0:T(8,128)S(1)} %copy.10.need_ref, bf16[10496,128]{1,0:T(8,128)(2,1)S(1)} %convert_element_type.38.x_ref, bf16[20,128,512]{2,1,0:T(8,128)(2,1)S(1)} %bitcast.16), custom_call_target="tpu_custom_call" | custom-call | flops 83886080 | bytes 1048576 | tf_op jit(solution)/shard_map/pallas_call | solution.py:131
  45.6 0.0 copy-start.4
  45.6 0.0 copy-start.2
  45.6 0.0 copy-start.3
  45.6 2.1 %collective-permute-start = (f16[640,128]{1,0:T(8,128)(2,1)S(1)}, f16[640,128]{1,0:T(8,128)(2,1)S(1)}, u32[]{:S(2)}, u32[]{:S(2)}) collective-permute-start(f16[640,128]{1,0:T(8,128)(2,1)S(1)} %convert_element_type.42), channel_id=1, source_target_pairs={{0,1},{1,2},{2,3},{3,4},{4,5},{5,6},{6,7},{7,8},{8,9},{9,10},{10,1... | collective-permute-start | bytes 491528 | tf_op jit(solution)/shard_map/ppermute | solution.py:18
  47.7 1.6 %shard_map.83 = (f32[640,128]{1,0:T(8,128)S(1)}, f32[640,128]{1,0:T(8,128)S(1)}) custom-call(s32[5,20]{1,0:T(8,128)S(1)} %get-tuple-element.10.plan_ref, s32[16,2]{1,0:T(8,128)S(1)} %copy.10.need_ref, bf16[10496,128]{1,0:T(8,128)(2,1)S(1)} %convert_element_type.38.x_ref, bf16[20,128,512]{2,1,0:T(8,128)(2,1)S(1)} %bitcast.17), custom_call_target="tpu_custom_call" | custom-call | flops 167772160 | bytes 2097152 | tf_op jit(solution)/shard_map/pallas_call | solution.py:131
  49.3 5.5 %collective-permute-done.1 = f16[640,128]{1,0:T(8,128)(2,1)S(1)} collective-permute-done((f16[640,128]{1,0:T(8,128)(2,1)S(1)}, f16[640,128]{1,0:T(8,128)(2,1)S(1)}, u32[]{:S(2)}, u32[]{:S(2)}) %collective-permute-start.1) | collective-permute-done | bytes 163872 | tf_op jit(solution)/shard_map/ppermute | solution.py:18
  54.9 1.9 %collective-permute-start.2 = (f16[640,128]{1,0:T(8,128)(2,1)S(1)}, f16[640,128]{1,0:T(8,128)(2,1)S(1)}, u32[]{:S(2)}, u32[]{:S(2)}) collective-permute-start(f16[640,128]{1,0:T(8,128)(2,1)S(1)} %add_convert_fusion), channel_id=1, source_target_pairs={{0,2},{1,3},{2,4},{3,5},{4,6},{5,7},{6,8},{7,9},{8,10},{9,11},{10,... | collective-permute-start | bytes 491528 | tf_op jit(solution)/shard_map/ppermute | solution.py:18
  56.8 0.0 copy-done
  56.8 0.0 copy-done.4
  56.8 0.2 fusion.self_ref
  57.1 1.4 %collective-permute-done = f16[640,128]{1,0:T(8,128)(2,1)S(1)} collective-permute-done((f16[640,128]{1,0:T(8,128)(2,1)S(1)}, f16[640,128]{1,0:T(8,128)(2,1)S(1)}, u32[]{:S(2)}, u32[]{:S(2)}) %collective-permute-start) | collective-permute-done | bytes 163872 | tf_op jit(solution)/shard_map/ppermute | solution.py:18
  58.5 9.5 %collective-permute-done.2 = f16[640,128]{1,0:T(8,128)(2,1)S(1)} collective-permute-done((f16[640,128]{1,0:T(8,128)(2,1)S(1)}, f16[640,128]{1,0:T(8,128)(2,1)S(1)}, u32[]{:S(2)}, u32[]{:S(2)}) %collective-permute-start.2) | collective-permute-done | bytes 163872 | tf_op jit(solution)/shard_map/ppermute | solution.py:18
  68.1 0.0 copy-done.2
  68.1 0.0 copy-done.3
  68.1 1.0 %shard_map.86 = bf16[640,256]{1,0:T(8,128)(2,1)} custom-call(f32[640,256]{1,0:T(8,128)S(1)} %fusion.self_ref, f32[640,128]{1,0:T(8,128)S(1)} %get-tuple-element.12.rest_0_, f32[640,128]{1,0:T(8,128)S(1)} %convert_element_type.43.rest_1_, f32[640,128]{1,0:T(8,128)S(1)} %convert_element_type.47.rest_2_, bf16[128,256]{1,0:T(8,128)(2,1)S(1)} %copy-done.2, ...), custom_call_target="tpu_custom_call" | custom-call | tf_op jit(solution)/shard_map/pallas_call | solution.py:149
  (8 shorter events, 0.2 us)
Async XLA Ops:
  0.0 56.8 %copy-start = (bf16[128,256]{1,0:T(8,128)(2,1)S(1)}, bf16[128,256]{1,0:T(8,128)(2,1)}, u32[]{:S(2)}) copy-start(bf16[128,256]{1,0:T(8,128)(2,1)} %param.13) | copy-start | bytes 196612
  41.1 3.2 %copy-start.1 = (bf16[1,1,20,128,512]{4,3,2,1,0:T(8,128)(2,1)S(1)}, bf16[1,1,20,128,512]{4,3,2,1,0:T(8,128)(2,1)}, u32[]{:S(2)}) copy-start(bf16[1,1,20,128,512]{4,3,2,1,0:T(8,128)(2,1)} %param.12) | copy-start | bytes 7864324
  42.4 12.5 %collective-permute-start.1 = (f16[640,128]{1,0:T(8,128)(2,1)S(1)}, f16[640,128]{1,0:T(8,128)(2,1)S(1)}, u32[]{:S(2)}, u32[]{:S(2)}) collective-permute-start(f16[640,128]{1,0:T(8,128)(2,1)S(1)} %convert_element_type.44), channel_id=1, source_target_pairs={{0,1},{1,2},{2,3},{3,4},{4,5},{5,6},{6,7},{7,8},{8,9},{9,10},{10,1... | collective-permute-start | bytes 491528 | tf_op jit(solution)/shard_map/ppermute | solution.py:18
  45.6 11.2 %copy-start.4 = (bf16[640,128]{1,0:T(8,128)(2,1)S(1)}, bf16[640,128]{1,0:T(8,128)(2,1)}, u32[]{:S(2)}) copy-start(bf16[640,128]{1,0:T(8,128)(2,1)} %features_ref.1) | copy-start | bytes 491524
  45.6 22.5 %copy-start.2 = (bf16[128,256]{1,0:T(8,128)(2,1)S(1)}, bf16[128,256]{1,0:T(8,128)(2,1)}, u32[]{:S(2)}) copy-start(bf16[128,256]{1,0:T(8,128)(2,1)} %rest_3_.1) | copy-start | bytes 196612
  45.6 22.5 %copy-start.3 = (f32[256]{0:T(256)S(1)}, f32[256]{0:T(256)}, u32[]{:S(2)}) copy-start(f32[256]{0:T(256)} %param.15) | copy-start | bytes 3076
  45.6 12.9 %collective-permute-start = (f16[640,128]{1,0:T(8,128)(2,1)S(1)}, f16[640,128]{1,0:T(8,128)(2,1)S(1)}, u32[]{:S(2)}, u32[]{:S(2)}) collective-permute-start(f16[640,128]{1,0:T(8,128)(2,1)S(1)} %convert_element_type.42), channel_id=1, source_target_pairs={{0,1},{1,2},{2,3},{3,4},{4,5},{5,6},{6,7},{7,8},{8,9},{9,10},{10,1... | collective-permute-start | bytes 491528 | tf_op jit(solution)/shard_map/ppermute | solution.py:18
  54.9 13.1 %collective-permute-start.2 = (f16[640,128]{1,0:T(8,128)(2,1)S(1)}, f16[640,128]{1,0:T(8,128)(2,1)S(1)}, u32[]{:S(2)}, u32[]{:S(2)}) collective-permute-start(f16[640,128]{1,0:T(8,128)(2,1)S(1)} %add_convert_fusion), channel_id=1, source_target_pairs={{0,2},{1,3},{2,4},{3,5},{4,6},{5,7},{6,8},{7,9},{8,10},{9,11},{10,... | collective-permute-start | bytes 491528 | tf_op jit(solution)/shard_map/ppermute | solution.py:18

commit v3 on v2

--- a/solution.py
+++ b/solution.py
@@ -10,11 +10,12 @@
 SCALE = 8192.0
 PART_SCALE = 32.0
 VMEM_LIMIT = 8 * 2**20
+LINE = 8
 
 
-def passed_along(value, axis, steps):
+def passed_along(value, axis, steps, chosen=lambda source: True):
     count = lax.axis_size(axis)
-    pairs = [(source, (source + steps) % count) for source in range(count)]
+    pairs = [(source, (source + steps) % count) for source in range(count) if chosen(source)]
     return lax.ppermute(value, axis, pairs)
 
 
@@ -44,23 +45,22 @@
         copy.wait()
 
 
-def band_kernel(ks, first, own, rows, held, plan_ref, need_ref, x_ref, adj_ref, *rest):
-    *outs, operand = rest
+def band_kernel(ks, first, own, rows, held, plan_ref, need_ref, x_ref, adj_ref, *outs):
     per_dst = plan_ref.shape[0] - 1
     cap = need_ref.shape[1]
     for k, out_ref in zip(ks, outs, strict=True):
         for b in range(own):
             block = k * own + b
+            tiles = []
             for j in range(per_dst):
                 slot = plan_ref[j, block]
                 owner = lax.div(slot, cap)
                 wanted = jnp.clip(need_ref[owner, lax.rem(slot, cap)], 0, own - 1)
                 start = pl.multiple_of(owner * held + wanted * rows, 16)
                 tile = x_ref[pl.ds(start, rows), :]
-                tile = jnp.where(j < plan_ref[per_dst, block], tile, jnp.zeros_like(tile))
-                operand[b, j * rows : (j + 1) * rows, :] = tile
-        for b in range(own):
-            product = jnp.dot(adj_ref[k * own + b - first], operand[b], preferred_element_type=jnp.float32)
+                tiles.append(jnp.where(j < plan_ref[per_dst, block], tile, jnp.zeros_like(tile)))
+            operand = jnp.concatenate(tiles, axis=0)
+            product = jnp.dot(adj_ref[block - first], operand, preferred_element_type=jnp.float32)
             out_ref[b * rows : (b + 1) * rows, :] = product * (PART_SCALE / SCALE)
 
 
@@ -126,26 +126,31 @@
     need = (need.reshape(row_count, cap).astype(jnp.float32) * (1.0 / SCALE)).astype(jnp.int32)
     tile_flops = 2 * rows * rows * per_dst * width
 
-    def products(ks, matrices, first):
+    def products(ks, matrices, first, need):
         count = len(ks) * own
         return pl.pallas_call(
             functools.partial(band_kernel, ks, first, own, rows, held),
             out_shape=[pltpu.VMEM((nodes, width), jnp.float32)] * len(ks),
             in_specs=[smem, smem, vmem, vmem],
             out_specs=[vmem] * len(ks),
-            scratch_shapes=[pltpu.VMEM((own, per_dst * rows, width), jnp.bfloat16)],
             compiler_params=params,
             cost_estimate=pl.CostEstimate(flops=count * tile_flops, bytes_accessed=len(ks) * 2**20, transcendentals=0),
         )(plan, need, in_vmem(source), in_vmem(matrices))
 
-    (far,) = products((3,), adjacent_last, last)
-    far = passed_along(far.astype(jnp.float16), "col", 1)
-    (near,) = products((1,), adjacent, 0)
+    (far,) = products((3,), adjacent_last, last, need)
+    far = far.astype(jnp.float16)
+    stayed = passed_along(far, "col", 1, lambda source: source % LINE < LINE - 1)
+    left = passed_along(far, "col", 1, lambda source: source % LINE == LINE - 1)
+    (near,) = products((1,), adjacent, 0, need)
     near = passed_along(near.astype(jnp.float16), "col", 1)
-    mid, mine = products((2, 0), adjacent, 0)
-    far = passed_along((far.astype(jnp.float32) + mid).astype(jnp.float16), "col", 2)
-    parts = (mine, near.astype(jnp.float32), far.astype(jnp.float32))
+    mid, mine = products((2, 0), adjacent, 0, need)
+    pair = (stayed.astype(jnp.float32) + mid).astype(jnp.float16)
+    crossing = passed_along(pair, "col", 2, lambda source: source % LINE >= LINE - 2)
     own_part = jnp.dot(features, w_self, preferred_element_type=jnp.float32)
+    left, pair = lax.optimization_barrier((left, pair))
+    pair = (stayed.astype(jnp.float32) + left.astype(jnp.float32) + mid).astype(jnp.float16)
+    inside = passed_along(pair, "col", 2, lambda source: source % LINE < LINE - 2)
+    parts = (mine, near.astype(jnp.float32), crossing.astype(jnp.float32) + inside.astype(jnp.float32))
     return pl.pallas_call(
         final_kernel,
         out_shape=jax.ShapeDtypeStruct((nodes, w_self.shape[1]), jnp.bfloat16),

time: 69.3 us -> 66.5 us (0.960); the launches traced: 69.1 us -> 65.4 us
  waiting for transfers between devices: 16.5 us -> 11.8 us
  starting transfers between devices: 5.89 us -> 7.24 us
    ppermute x3 -> x5, waiting for transfers between devices: 16.5 us -> 11.8 us  [passed_along(): return lax.ppermute(value, axis, pairs)]
    ppermute x3 -> x5, starting transfers between devices: 5.89 us -> 7.24 us  [passed_along(): return lax.ppermute(value, axis, pairs)]
  transfers between devices with their start and end apart: 3 -> 5, of which waited for: 3 -> 4; matrix products, arithmetic and copies ran while one was open for 0% -> 1% of each run, Pallas kernels for 4% -> 4%
where the time goes in v3:
time: 66.5 us; the launch traced here: 65.4 us
  blocking collectives  39.2 us (59%)
  waiting for transfers between devices  11.8 us (18%)
  starting transfers between devices  7.24 us (11%)
  Pallas kernels  5.86 us (9%)
    all_gather x1, blocking collectives, shards(): got = lax.all_gather(sent, 'row', axis=0, tiled=True)  39.2 us
    ppermute x5, waiting for transfers between devices, passed_along(): return lax.ppermute(value, axis, pairs)  11.8 us
    ppermute x5, starting transfers between devices, passed_along(): return lax.ppermute(value, axis, pairs)  7.24 us
    pallas_call x3, Pallas kernels, products(): pl.pallas_call(functools.partial(band_kernel, ks, first, own, rows, held)...  3.6 us
  transfers between devices with their start and end apart: 5, of which 4 were waited for; matrix products, arithmetic and copies ran while one was open for 1% of the time, Pallas kernels for 4%

profile of v3, /device:TPU:1, one launch (start us, length us, event | category | flops | bytes accessed | tf_op | source)
XLA Modules:
  0.0 65.4 jit_solution(7946325005706332895)
XLA Ops:
  0.0 0.0 copy-start
  0.0 1.3 %shard_map.82 = (bf16[656,128]{1,0:T(8,128)(2,1)S(1)}, s32[5,20]{1,0:T(8,128)S(1)}, bf16[5,128,512]{2,1,0:T(8,128)(2,1)S(1)}) custom-call(bf16[640,128]{1,0:T(8,128)(2,1)} %features_ref.1, s32[2,16]{1,0:T(2,128)} %bitcast.20, s32[4,20]{1,0:T(4,128)} %bitcast.19, s32[1,20]{1,0:T(1,128)} %bitcast.21, bf16[20,128,512]{2,1,0:T(8,128)(2,1)} %bitcast.15), custom_call_target="tpu_custom_call" | custom-call | tf_op jit(solution)/shard_map/pallas_call | solution.py:103
  1.4 39.2 %all-gather.1 = f16[10496,128]{1,0:T(8,128)(2,1)S(1)} all-gather(f16[656,128]{1,0:T(8,128)(2,1)S(1)} %multiply_convert_fusion), channel_id=1, replica_groups=mesh['row'=16,'col'=64] {'row'}, dimensions={0}, use_global_device_ids=true | all-gather | bytes 2854912 | tf_op jit(solution)/shard_map/all_gather | solution.py:122
  40.5 0.3 convert_element_type.48.x_ref
  40.9 0.1 copy.13
  41.0 0.1 copy.10.need_ref
  41.1 0.0 copy-start.1
  41.1 1.1 %shard_map.85 = f32[640,128]{1,0:T(8,128)S(1)} custom-call(s32[5,20]{1,0:T(8,128)S(1)} %get-tuple-element.11.plan_ref, s32[16,2]{1,0:T(8,128)S(1)} %copy.10.need_ref, bf16[10496,128]{1,0:T(8,128)(2,1)S(1)} %convert_element_type.48.x_ref, bf16[5,128,512]{2,1,0:T(8,128)(2,1)S(1)} %get-tuple-element.14.adj_ref), custom_call_target="tpu_custom_call" | custom-call | flops 83886080 | bytes 1048576 | tf_op jit(solution)/shard_map/pallas_call | solution.py:131
  42.3 1.3 %collective-permute-start.1 = (f16[640,128]{1,0:T(8,128)(2,1)S(1)}, f16[640,128]{1,0:T(8,128)(2,1)S(1)}, u32[]{:S(2)}, u32[]{:S(2)}) collective-permute-start(f16[640,128]{1,0:T(8,128)(2,1)S(1)} %convert_element_type.54), channel_id=1, source_target_pairs={{0,1},{1,2},{2,3},{3,4},{4,5},{5,6},{6,7},{8,9},{9,10},{10,11},{11... | collective-permute-start | bytes 491528 | tf_op jit(solution)/shard_map/ppermute | solution.py:19
  43.6 1.3 %collective-permute-start.3 = (f16[640,128]{1,0:T(8,128)(2,1)S(1)}, f16[640,128]{1,0:T(8,128)(2,1)S(1)}, u32[]{:S(2)}, u32[]{:S(2)}) collective-permute-start(f16[640,128]{1,0:T(8,128)(2,1)S(1)} %convert_element_type.54), channel_id=1, source_target_pairs={{7,8},{15,16},{23,24},{31,32},{39,40},{47,48},{55,56},{63,0},{71,7... | collective-permute-start | bytes 491528 | tf_op jit(solution)/shard_map/ppermute | solution.py:19
  44.9 0.0 copy-done.1
  44.9 1.1 %shard_map.84 = f32[640,128]{1,0:T(8,128)S(1)} custom-call(s32[5,20]{1,0:T(8,128)S(1)} %get-tuple-element.11.plan_ref, s32[16,2]{1,0:T(8,128)S(1)} %copy.10.need_ref, bf16[10496,128]{1,0:T(8,128)(2,1)S(1)} %convert_element_type.48.x_ref, bf16[20,128,512]{2,1,0:T(8,128)(2,1)S(1)} %bitcast.16), custom_call_target="tpu_custom_call" | custom-call | flops 83886080 | bytes 1048576 | tf_op jit(solution)/shard_map/pallas_call | solution.py:131
  46.0 0.0 copy-start.4
  46.1 2.1 %collective-permute-start = (f16[640,128]{1,0:T(8,128)(2,1)S(1)}, f16[640,128]{1,0:T(8,128)(2,1)S(1)}, u32[]{:S(2)}, u32[]{:S(2)}) collective-permute-start(f16[640,128]{1,0:T(8,128)(2,1)S(1)} %convert_element_type.52), channel_id=1, source_target_pairs={{0,1},{1,2},{2,3},{3,4},{4,5},{5,6},{6,7},{7,8},{8,9},{9,10},{10,1... | collective-permute-start | bytes 491528 | tf_op jit(solution)/shard_map/ppermute | solution.py:19
  48.1 1.3 %shard_map.83 = (f32[640,128]{1,0:T(8,128)S(1)}, f32[640,128]{1,0:T(8,128)S(1)}) custom-call(s32[5,20]{1,0:T(8,128)S(1)} %get-tuple-element.11.plan_ref, s32[16,2]{1,0:T(8,128)S(1)} %copy.10.need_ref, bf16[10496,128]{1,0:T(8,128)(2,1)S(1)} %convert_element_type.48.x_ref, bf16[20,128,512]{2,1,0:T(8,128)(2,1)S(1)} %bitcast.17), custom_call_target="tpu_custom_call" | custom-call | flops 167772160 | bytes 2097152 | tf_op jit(solution)/shard_map/pallas_call | solution.py:131
  49.5 0.0 copy-start.2
  49.5 0.0 copy-start.3
  49.5 0.0 collective-permute-done.1
  49.5 0.1 fusion
  49.6 1.3 %collective-permute-start.2 = (f16[640,128]{1,0:T(8,128)(2,1)S(1)}, f16[640,128]{1,0:T(8,128)(2,1)S(1)}, u32[]{:S(2)}, u32[]{:S(2)}) collective-permute-start(f16[640,128]{1,0:T(8,128)(2,1)S(1)} %fusion), channel_id=1, source_target_pairs={{6,8},{7,9},{14,16},{15,17},{22,24},{23,25},{30,32},{31,33},{38,40... | collective-permute-start | bytes 491528 | tf_op jit(solution)/shard_map/ppermute | solution.py:19
  50.9 4.5 %collective-permute-done.3 = f16[640,128]{1,0:T(8,128)(2,1)S(1)} collective-permute-done((f16[640,128]{1,0:T(8,128)(2,1)S(1)}, f16[640,128]{1,0:T(8,128)(2,1)S(1)}, u32[]{:S(2)}, u32[]{:S(2)}) %collective-permute-start.3) | collective-permute-done | bytes 163872 | tf_op jit(solution)/shard_map/ppermute | solution.py:19
  55.4 0.1 fusion.2
  55.5 1.3 %collective-permute-start.4 = (f16[640,128]{1,0:T(8,128)(2,1)S(1)}, f16[640,128]{1,0:T(8,128)(2,1)S(1)}, u32[]{:S(2)}, u32[]{:S(2)}) collective-permute-start(f16[640,128]{1,0:T(8,128)(2,1)S(1)} %fusion.2), channel_id=1, source_target_pairs={{0,2},{1,3},{2,4},{3,5},{4,6},{5,7},{8,10},{9,11},{10,12},{11,13},... | collective-permute-start | bytes 491528 | tf_op jit(solution)/shard_map/ppermute | solution.py:19
  56.8 0.0 copy-done
  56.8 0.0 copy-done.4
  56.8 0.2 fusion.3.self_ref
  57.0 2.0 %collective-permute-done = f16[640,128]{1,0:T(8,128)(2,1)S(1)} collective-permute-done((f16[640,128]{1,0:T(8,128)(2,1)S(1)}, f16[640,128]{1,0:T(8,128)(2,1)S(1)}, u32[]{:S(2)}, u32[]{:S(2)}) %collective-permute-start) | collective-permute-done | bytes 163872 | tf_op jit(solution)/shard_map/ppermute | solution.py:19
  59.1 0.6 collective-permute-done.4
  59.7 4.7 %collective-permute-done.2 = f16[640,128]{1,0:T(8,128)(2,1)S(1)} collective-permute-done((f16[640,128]{1,0:T(8,128)(2,1)S(1)}, f16[640,128]{1,0:T(8,128)(2,1)S(1)}, u32[]{:S(2)}, u32[]{:S(2)}) %collective-permute-start.2) | collective-permute-done | bytes 163872 | tf_op jit(solution)/shard_map/ppermute | solution.py:19
  64.4 0.0 copy-done.2
  64.4 0.0 copy-done.3
  64.4 1.0 %shard_map.86 = bf16[640,256]{1,0:T(8,128)(2,1)} custom-call(f32[640,256]{1,0:T(8,128)S(1)} %fusion.3.self_ref, f32[640,128]{1,0:T(8,128)S(1)} %get-tuple-element.13.rest_0_, f32[640,128]{1,0:T(8,128)S(1)} %convert_element_type.53.rest_1_, f32[640,128]{1,0:T(8,128)S(1)} %convert_add_fusion.2.rest_2_, bf16[128,256]{1,0:T(8,128)(2,1)S(1)} %copy-done.2, ...), custom_call_target="tpu_custom_call" | custom-call | tf_op jit(solution)/shard_map/pallas_call | solution.py:154
  (7 shorter events, 0.2 us)
Async XLA Ops:
  0.0 56.8 %copy-start = (bf16[128,256]{1,0:T(8,128)(2,1)S(1)}, bf16[128,256]{1,0:T(8,128)(2,1)}, u32[]{:S(2)}) copy-start(bf16[128,256]{1,0:T(8,128)(2,1)} %param.13) | copy-start | bytes 196612
  41.1 3.8 %copy-start.1 = (bf16[1,1,20,128,512]{4,3,2,1,0:T(8,128)(2,1)S(1)}, bf16[1,1,20,128,512]{4,3,2,1,0:T(8,128)(2,1)}, u32[]{:S(2)}) copy-start(bf16[1,1,20,128,512]{4,3,2,1,0:T(8,128)(2,1)} %param.12) | copy-start | bytes 7864324
  42.3 7.2 %collective-permute-start.1 = (f16[640,128]{1,0:T(8,128)(2,1)S(1)}, f16[640,128]{1,0:T(8,128)(2,1)S(1)}, u32[]{:S(2)}, u32[]{:S(2)}) collective-permute-start(f16[640,128]{1,0:T(8,128)(2,1)S(1)} %convert_element_type.54), channel_id=1, source_target_pairs={{0,1},{1,2},{2,3},{3,4},{4,5},{5,6},{6,7},{8,9},{9,10},{10,11},{11... | collective-permute-start | bytes 491528 | tf_op jit(solution)/shard_map/ppermute | solution.py:19
  43.6 11.8 %collective-permute-start.3 = (f16[640,128]{1,0:T(8,128)(2,1)S(1)}, f16[640,128]{1,0:T(8,128)(2,1)S(1)}, u32[]{:S(2)}, u32[]{:S(2)}) collective-permute-start(f16[640,128]{1,0:T(8,128)(2,1)S(1)} %convert_element_type.54), channel_id=1, source_target_pairs={{7,8},{15,16},{23,24},{31,32},{39,40},{47,48},{55,56},{63,0},{71,7... | collective-permute-start | bytes 491528 | tf_op jit(solution)/shard_map/ppermute | solution.py:19
  46.0 10.8 %copy-start.4 = (bf16[640,128]{1,0:T(8,128)(2,1)S(1)}, bf16[640,128]{1,0:T(8,128)(2,1)}, u32[]{:S(2)}) copy-start(bf16[640,128]{1,0:T(8,128)(2,1)} %features_ref.1) | copy-start | bytes 491524
  46.1 13.0 %collective-permute-start = (f16[640,128]{1,0:T(8,128)(2,1)S(1)}, f16[640,128]{1,0:T(8,128)(2,1)S(1)}, u32[]{:S(2)}, u32[]{:S(2)}) collective-permute-start(f16[640,128]{1,0:T(8,128)(2,1)S(1)} %convert_element_type.52), channel_id=1, source_target_pairs={{0,1},{1,2},{2,3},{3,4},{4,5},{5,6},{6,7},{7,8},{8,9},{9,10},{10,1... | collective-permute-start | bytes 491528 | tf_op jit(solution)/shard_map/ppermute | solution.py:19
  49.5 14.9 %copy-start.2 = (bf16[128,256]{1,0:T(8,128)(2,1)S(1)}, bf16[128,256]{1,0:T(8,128)(2,1)}, u32[]{:S(2)}) copy-start(bf16[128,256]{1,0:T(8,128)(2,1)} %rest_3_.1) | copy-start | bytes 196612
  49.5 14.9 %copy-start.3 = (f32[256]{0:T(256)S(1)}, f32[256]{0:T(256)}, u32[]{:S(2)}) copy-start(f32[256]{0:T(256)} %param.15) | copy-start | bytes 3076
  49.6 14.8 %collective-permute-start.2 = (f16[640,128]{1,0:T(8,128)(2,1)S(1)}, f16[640,128]{1,0:T(8,128)(2,1)S(1)}, u32[]{:S(2)}, u32[]{:S(2)}) collective-permute-start(f16[640,128]{1,0:T(8,128)(2,1)S(1)} %fusion), channel_id=1, source_target_pairs={{6,8},{7,9},{14,16},{15,17},{22,24},{23,25},{30,32},{31,33},{38,40... | collective-permute-start | bytes 491528 | tf_op jit(solution)/shard_map/ppermute | solution.py:19
  55.5 4.2 %collective-permute-start.4 = (f16[640,128]{1,0:T(8,128)(2,1)S(1)}, f16[640,128]{1,0:T(8,128)(2,1)S(1)}, u32[]{:S(2)}, u32[]{:S(2)}) collective-permute-start(f16[640,128]{1,0:T(8,128)(2,1)S(1)} %fusion.2), channel_id=1, source_target_pairs={{0,2},{1,3},{2,4},{3,5},{4,6},{5,7},{8,10},{9,11},{10,12},{11,13},... | collective-permute-start | bytes 491528 | tf_op jit(solution)/shard_map/ppermute | solution.py:19

commit v4 on v3

--- a/solution.py
+++ b/solution.py
@@ -45,9 +45,8 @@
         copy.wait()
 
 
-def band_kernel(ks, first, own, rows, held, plan_ref, need_ref, x_ref, adj_ref, *outs):
+def band_kernel(ks, first, own, rows, held, cap, plan_ref, need_ref, x_ref, adj_ref, *outs):
     per_dst = plan_ref.shape[0] - 1
-    cap = need_ref.shape[1]
     for k, out_ref in zip(ks, outs, strict=True):
         for b in range(own):
             block = k * own + b
@@ -122,14 +121,14 @@
     got = lax.all_gather(sent, "row", axis=0, tiled=True)
     source = got.astype(jnp.bfloat16)
     reader = lax.axis_index("row")
-    need = lax.dynamic_slice(source.reshape(row_count, held, width), (0, nodes + reader, 0), (row_count, 1, cap))
-    need = (need.reshape(row_count, cap).astype(jnp.float32) * (1.0 / SCALE)).astype(jnp.int32)
+    need = lax.dynamic_slice(source.reshape(row_count, held, width), (0, nodes + reader, 0), (row_count, 1, width))
+    need = (need.reshape(row_count, width).astype(jnp.float32) * (1.0 / SCALE)).astype(jnp.int32)
     tile_flops = 2 * rows * rows * per_dst * width
 
     def products(ks, matrices, first, need):
         count = len(ks) * own
         return pl.pallas_call(
-            functools.partial(band_kernel, ks, first, own, rows, held),
+            functools.partial(band_kernel, ks, first, own, rows, held, cap),
             out_shape=[pltpu.VMEM((nodes, width), jnp.float32)] * len(ks),
             in_specs=[smem, smem, vmem, vmem],
             out_specs=[vmem] * len(ks),

time: 66.5 us -> 66.4 us (level)
  no operation moved by 1% of the time
where the time goes in v4:
time: 66.4 us; the launch traced here: 65.2 us
  blocking collectives  39.2 us (59%)
  waiting for transfers between devices  11.8 us (18%)
  starting transfers between devices  7.24 us (11%)
  Pallas kernels  5.87 us (9%)
    all_gather x1, blocking collectives, shards(): got = lax.all_gather(sent, 'row', axis=0, tiled=True)  39.2 us
    ppermute x5, waiting for transfers between devices, passed_along(): return lax.ppermute(value, axis, pairs)  11.8 us
    ppermute x5, starting transfers between devices, passed_along(): return lax.ppermute(value, axis, pairs)  7.24 us
    pallas_call x3, Pallas kernels, products(): pl.pallas_call(functools.partial(band_kernel, ks, first, own, rows, held,...  3.61 us
  transfers between devices with their start and end apart: 5, of which 4 were waited for; matrix products, arithmetic and copies ran while one was open for 1% of the time, Pallas kernels for 4%

profile of v4, /device:TPU:1, one launch (start us, length us, event | category | flops | bytes accessed | tf_op | source)
XLA Modules:
  0.0 65.2 jit_solution(14629326693835594247)
XLA Ops:
  0.0 0.0 copy-start
  0.0 1.3 %shard_map.82 = (bf16[656,128]{1,0:T(8,128)(2,1)S(1)}, s32[5,20]{1,0:T(8,128)S(1)}, bf16[5,128,512]{2,1,0:T(8,128)(2,1)S(1)}) custom-call(bf16[640,128]{1,0:T(8,128)(2,1)} %features_ref.1, s32[2,16]{1,0:T(2,128)} %bitcast.20, s32[4,20]{1,0:T(4,128)} %bitcast.19, s32[1,20]{1,0:T(1,128)} %bitcast.21, bf16[20,128,512]{2,1,0:T(8,128)(2,1)} %bitcast.15), custom_call_target="tpu_custom_call" | custom-call | tf_op jit(solution)/shard_map/pallas_call | solution.py:102
  1.4 39.2 %all-gather.1 = f16[10496,128]{1,0:T(8,128)(2,1)S(1)} all-gather(f16[656,128]{1,0:T(8,128)(2,1)S(1)} %multiply_convert_fusion), channel_id=1, replica_groups=mesh['row'=16,'col'=64] {'row'}, dimensions={0}, use_global_device_ids=true | all-gather | bytes 2854912 | tf_op jit(solution)/shard_map/all_gather | solution.py:121
  40.5 0.3 convert_element_type.48.x_ref
  40.9 0.0 copy-start.1
  40.9 1.1 %shard_map.85 = f32[640,128]{1,0:T(8,128)S(1)} custom-call(s32[5,20]{1,0:T(8,128)S(1)} %get-tuple-element.11.plan_ref, s32[16,128]{1,0:T(8,128)S(1)} %convert_bitcast_fusion.need_ref, bf16[10496,128]{1,0:T(8,128)(2,1)S(1)} %convert_element_type.48.x_ref, bf16[5,128,512]{2,1,0:T(8,128)(2,1)S(1)} %get-tuple-element.14.adj_ref), custom_call_target="tpu_custom_call" | custom-call | flops 83886080 | bytes 1048576 | tf_op jit(solution)/shard_map/pallas_call | solution.py:130
  42.1 1.3 %collective-permute-start.1 = (f16[640,128]{1,0:T(8,128)(2,1)S(1)}, f16[640,128]{1,0:T(8,128)(2,1)S(1)}, u32[]{:S(2)}, u32[]{:S(2)}) collective-permute-start(f16[640,128]{1,0:T(8,128)(2,1)S(1)} %convert_element_type.54), channel_id=1, source_target_pairs={{0,1},{1,2},{2,3},{3,4},{4,5},{5,6},{6,7},{8,9},{9,10},{10,11},{11... | collective-permute-start | bytes 491528 | tf_op jit(solution)/shard_map/ppermute | solution.py:19
  43.4 1.3 %collective-permute-start.3 = (f16[640,128]{1,0:T(8,128)(2,1)S(1)}, f16[640,128]{1,0:T(8,128)(2,1)S(1)}, u32[]{:S(2)}, u32[]{:S(2)}) collective-permute-start(f16[640,128]{1,0:T(8,128)(2,1)S(1)} %convert_element_type.54), channel_id=1, source_target_pairs={{7,8},{15,16},{23,24},{31,32},{39,40},{47,48},{55,56},{63,0},{71,7... | collective-permute-start | bytes 491528 | tf_op jit(solution)/shard_map/ppermute | solution.py:19
  44.7 0.0 copy-done.1
  44.7 1.1 %shard_map.84 = f32[640,128]{1,0:T(8,128)S(1)} custom-call(s32[5,20]{1,0:T(8,128)S(1)} %get-tuple-element.11.plan_ref, s32[16,128]{1,0:T(8,128)S(1)} %convert_bitcast_fusion.need_ref, bf16[10496,128]{1,0:T(8,128)(2,1)S(1)} %convert_element_type.48.x_ref, bf16[20,128,512]{2,1,0:T(8,128)(2,1)S(1)} %bitcast.16), custom_call_target="tpu_custom_call" | custom-call | flops 83886080 | bytes 1048576 | tf_op jit(solution)/shard_map/pallas_call | solution.py:130
  45.9 0.0 copy-start.4
  45.9 2.1 %collective-permute-start = (f16[640,128]{1,0:T(8,128)(2,1)S(1)}, f16[640,128]{1,0:T(8,128)(2,1)S(1)}, u32[]{:S(2)}, u32[]{:S(2)}) collective-permute-start(f16[640,128]{1,0:T(8,128)(2,1)S(1)} %convert_element_type.52), channel_id=1, source_target_pairs={{0,1},{1,2},{2,3},{3,4},{4,5},{5,6},{6,7},{7,8},{8,9},{9,10},{10,1... | collective-permute-start | bytes 491528 | tf_op jit(solution)/shard_map/ppermute | solution.py:19
  47.9 1.3 %shard_map.83 = (f32[640,128]{1,0:T(8,128)S(1)}, f32[640,128]{1,0:T(8,128)S(1)}) custom-call(s32[5,20]{1,0:T(8,128)S(1)} %get-tuple-element.11.plan_ref, s32[16,128]{1,0:T(8,128)S(1)} %convert_bitcast_fusion.need_ref, bf16[10496,128]{1,0:T(8,128)(2,1)S(1)} %convert_element_type.48.x_ref, bf16[20,128,512]{2,1,0:T(8,128)(2,1)S(1)} %bitcast.17), custom_call_target="tpu_custom_call" | custom-call | flops 167772160 | bytes 2097152 | tf_op jit(solution)/shard_map/pallas_call | solution.py:130
  49.3 0.0 copy-start.2
  49.3 0.0 copy-start.3
  49.3 0.0 collective-permute-done.1
  49.3 0.1 fusion
  49.4 1.3 %collective-permute-start.2 = (f16[640,128]{1,0:T(8,128)(2,1)S(1)}, f16[640,128]{1,0:T(8,128)(2,1)S(1)}, u32[]{:S(2)}, u32[]{:S(2)}) collective-permute-start(f16[640,128]{1,0:T(8,128)(2,1)S(1)} %fusion), channel_id=1, source_target_pairs={{6,8},{7,9},{14,16},{15,17},{22,24},{23,25},{30,32},{31,33},{38,40... | collective-permute-start | bytes 491528 | tf_op jit(solution)/shard_map/ppermute | solution.py:19
  50.7 4.5 %collective-permute-done.3 = f16[640,128]{1,0:T(8,128)(2,1)S(1)} collective-permute-done((f16[640,128]{1,0:T(8,128)(2,1)S(1)}, f16[640,128]{1,0:T(8,128)(2,1)S(1)}, u32[]{:S(2)}, u32[]{:S(2)}) %collective-permute-start.3) | collective-permute-done | bytes 163872 | tf_op jit(solution)/shard_map/ppermute | solution.py:19
  55.2 0.1 fusion.2
  55.3 1.3 %collective-permute-start.4 = (f16[640,128]{1,0:T(8,128)(2,1)S(1)}, f16[640,128]{1,0:T(8,128)(2,1)S(1)}, u32[]{:S(2)}, u32[]{:S(2)}) collective-permute-start(f16[640,128]{1,0:T(8,128)(2,1)S(1)} %fusion.2), channel_id=1, source_target_pairs={{0,2},{1,3},{2,4},{3,5},{4,6},{5,7},{8,10},{9,11},{10,12},{11,13},... | collective-permute-start | bytes 491528 | tf_op jit(solution)/shard_map/ppermute | solution.py:19
  56.6 0.0 copy-done
  56.6 0.0 copy-done.4
  56.6 0.2 fusion.3.self_ref
  56.9 2.0 %collective-permute-done = f16[640,128]{1,0:T(8,128)(2,1)S(1)} collective-permute-done((f16[640,128]{1,0:T(8,128)(2,1)S(1)}, f16[640,128]{1,0:T(8,128)(2,1)S(1)}, u32[]{:S(2)}, u32[]{:S(2)}) %collective-permute-start) | collective-permute-done | bytes 163872 | tf_op jit(solution)/shard_map/ppermute | solution.py:19
  58.9 0.6 collective-permute-done.4
  59.5 4.6 %collective-permute-done.2 = f16[640,128]{1,0:T(8,128)(2,1)S(1)} collective-permute-done((f16[640,128]{1,0:T(8,128)(2,1)S(1)}, f16[640,128]{1,0:T(8,128)(2,1)S(1)}, u32[]{:S(2)}, u32[]{:S(2)}) %collective-permute-start.2) | collective-permute-done | bytes 163872 | tf_op jit(solution)/shard_map/ppermute | solution.py:19
  64.2 0.0 copy-done.2
  64.2 0.0 copy-done.3
  64.2 1.0 %shard_map.86 = bf16[640,256]{1,0:T(8,128)(2,1)} custom-call(f32[640,256]{1,0:T(8,128)S(1)} %fusion.3.self_ref, f32[640,128]{1,0:T(8,128)S(1)} %get-tuple-element.13.rest_0_, f32[640,128]{1,0:T(8,128)S(1)} %convert_element_type.53.rest_1_, f32[640,128]{1,0:T(8,128)S(1)} %convert_add_fusion.2.rest_2_, bf16[128,256]{1,0:T(8,128)(2,1)S(1)} %copy-done.2, ...), custom_call_target="tpu_custom_call" | custom-call | tf_op jit(solution)/shard_map/pallas_call | solution.py:153
  (7 shorter events, 0.2 us)
Async XLA Ops:
  0.0 56.6 %copy-start = (bf16[128,256]{1,0:T(8,128)(2,1)S(1)}, bf16[128,256]{1,0:T(8,128)(2,1)}, u32[]{:S(2)}) copy-start(bf16[128,256]{1,0:T(8,128)(2,1)} %param.13) | copy-start | bytes 196612
  40.9 3.8 %copy-start.1 = (bf16[1,1,20,128,512]{4,3,2,1,0:T(8,128)(2,1)S(1)}, bf16[1,1,20,128,512]{4,3,2,1,0:T(8,128)(2,1)}, u32[]{:S(2)}) copy-start(bf16[1,1,20,128,512]{4,3,2,1,0:T(8,128)(2,1)} %param.12) | copy-start | bytes 7864324
  42.1 7.2 %collective-permute-start.1 = (f16[640,128]{1,0:T(8,128)(2,1)S(1)}, f16[640,128]{1,0:T(8,128)(2,1)S(1)}, u32[]{:S(2)}, u32[]{:S(2)}) collective-permute-start(f16[640,128]{1,0:T(8,128)(2,1)S(1)} %convert_element_type.54), channel_id=1, source_target_pairs={{0,1},{1,2},{2,3},{3,4},{4,5},{5,6},{6,7},{8,9},{9,10},{10,11},{11... | collective-permute-start | bytes 491528 | tf_op jit(solution)/shard_map/ppermute | solution.py:19
  43.4 11.9 %collective-permute-start.3 = (f16[640,128]{1,0:T(8,128)(2,1)S(1)}, f16[640,128]{1,0:T(8,128)(2,1)S(1)}, u32[]{:S(2)}, u32[]{:S(2)}) collective-permute-start(f16[640,128]{1,0:T(8,128)(2,1)S(1)} %convert_element_type.54), channel_id=1, source_target_pairs={{7,8},{15,16},{23,24},{31,32},{39,40},{47,48},{55,56},{63,0},{71,7... | collective-permute-start | bytes 491528 | tf_op jit(solution)/shard_map/ppermute | solution.py:19
  45.9 10.8 %copy-start.4 = (bf16[640,128]{1,0:T(8,128)(2,1)S(1)}, bf16[640,128]{1,0:T(8,128)(2,1)}, u32[]{:S(2)}) copy-start(bf16[640,128]{1,0:T(8,128)(2,1)} %features_ref.1) | copy-start | bytes 491524
  45.9 13.0 %collective-permute-start = (f16[640,128]{1,0:T(8,128)(2,1)S(1)}, f16[640,128]{1,0:T(8,128)(2,1)S(1)}, u32[]{:S(2)}, u32[]{:S(2)}) collective-permute-start(f16[640,128]{1,0:T(8,128)(2,1)S(1)} %convert_element_type.52), channel_id=1, source_target_pairs={{0,1},{1,2},{2,3},{3,4},{4,5},{5,6},{6,7},{7,8},{8,9},{9,10},{10,1... | collective-permute-start | bytes 491528 | tf_op jit(solution)/shard_map/ppermute | solution.py:19
  49.3 14.9 %copy-start.2 = (bf16[128,256]{1,0:T(8,128)(2,1)S(1)}, bf16[128,256]{1,0:T(8,128)(2,1)}, u32[]{:S(2)}) copy-start(bf16[128,256]{1,0:T(8,128)(2,1)} %rest_3_.1) | copy-start | bytes 196612
  49.3 14.9 %copy-start.3 = (f32[256]{0:T(256)S(1)}, f32[256]{0:T(256)}, u32[]{:S(2)}) copy-start(f32[256]{0:T(256)} %param.15) | copy-start | bytes 3076
  49.4 14.8 %collective-permute-start.2 = (f16[640,128]{1,0:T(8,128)(2,1)S(1)}, f16[640,128]{1,0:T(8,128)(2,1)S(1)}, u32[]{:S(2)}, u32[]{:S(2)}) collective-permute-start(f16[640,128]{1,0:T(8,128)(2,1)S(1)} %fusion), channel_id=1, source_target_pairs={{6,8},{7,9},{14,16},{15,17},{22,24},{23,25},{30,32},{31,33},{38,40... | collective-permute-start | bytes 491528 | tf_op jit(solution)/shard_map/ppermute | solution.py:19
  55.3 4.2 %collective-permute-start.4 = (f16[640,128]{1,0:T(8,128)(2,1)S(1)}, f16[640,128]{1,0:T(8,128)(2,1)S(1)}, u32[]{:S(2)}, u32[]{:S(2)}) collective-permute-start(f16[640,128]{1,0:T(8,128)(2,1)S(1)} %fusion.2), channel_id=1, source_target_pairs={{0,2},{1,3},{2,4},{3,5},{4,6},{5,7},{8,10},{9,11},{10,12},{11,13},... | collective-permute-start | bytes 491528 | tf_op jit(solution)/shard_map/ppermute | solution.py:19
